TPU v7x, 32 devices: a whole 2x2x4 slice. The times are simulated.
32 devices in a mesh: cfg: 2 (over x), ta: 8 (over z, y), gz: 2 (over core).
Axes of the slice: x: 2, y: 2, z: 4, core: 2. Of those that a mesh axis runs over, the one named last changes fastest.
Arguments:
- links: float32 [16, 2, 72, 2304], P(('cfg', 'ta'), 'gz'), parts along dimension 0, may hold values from -1 to 1, as said below
Outputs:
- flowed: float32 [16, 2, 72, 2304], P(('cfg', 'ta'), 'gz'), parts along dimension 0
There are 2 independent parts, one for each index of `cfg`. A program takes and returns all parts, laid end to end along the dimension named above; each array names one. Nothing has to cross between parts.
Inputs may be any that keep to these rules, and one draw needn't show every extreme that they name: `links`: every link is a special unitary matrix (orthonormal rows, determinant one) up to rounding.
All inputs are finite; a program needn't handle non-finite values.
Results may differ from a plain program's by a relative error of at most 0.0001.
Values sent between devices are 32-bit elements; how exact they have to be, the bound alone decides.
A program may use at most 64 MiB of HBM per device.

v0:
```python
import jax
import jax.numpy as jnp
from jax import lax
from jax.sharding import PartitionSpec as P

X = 48


flow_step = 0.05


def with_halo(block, sides, width):
    for axis, dim in sides:
        count = lax.axis_size(axis)
        forward = [(i, i + 1) for i in range(count - 1)]
        forward.append((count - 1, 0))
        backward = [(target, source) for source, target in forward]
        low = lax.ppermute(
            lax.slice_in_dim(block, block.shape[dim] - width, None, axis=dim), axis, forward
        )
        high = lax.ppermute(lax.slice_in_dim(block, 0, width, axis=dim), axis, backward)
        block = jnp.concatenate([low, block, high], axis=dim)
    return block


def entry_row(row, column, part):
    return (row * 3 + column) * 2 + part


def multiply(left_factor, right_factor):
    entries = []
    for row in range(3):
        for column in range(3):
            real_sum = None
            imag_sum = None
            for inner in range(3):
                left_re = left_factor[..., entry_row(row, inner, 0), :]
                left_im = left_factor[..., entry_row(row, inner, 1), :]
                right_re = right_factor[..., entry_row(inner, column, 0), :]
                right_im = right_factor[..., entry_row(inner, column, 1), :]
                term_re = left_re * right_re - left_im * right_im
                term_im = left_re * right_im + left_im * right_re
                real_sum = term_re if real_sum is None else real_sum + term_re
                imag_sum = term_im if imag_sum is None else imag_sum + term_im
            entries.append(real_sum)
            entries.append(imag_sum)
    return jnp.stack(entries, axis=-2)


def dagger(matrix):
    entries = []
    for row in range(3):
        for column in range(3):
            entries.append(matrix[..., entry_row(column, row, 0), :])
            entries.append(-matrix[..., entry_row(column, row, 1), :])
    return jnp.stack(entries, axis=-2)


def diagonal_mask(part):
    values = [
        1.0 if position % 2 == part and position // 2 in (0, 4, 8) else 0.0
        for position in range(18)
    ]
    return jnp.array(values, jnp.float32)[:, None]


def project(loop_sum):
    antiherm = 0.5 * (loop_sum - dagger(loop_sum))
    trace_re = antiherm[..., 0, :] + antiherm[..., 8, :] + antiherm[..., 16, :]
    trace_im = antiherm[..., 1, :] + antiherm[..., 9, :] + antiherm[..., 17, :]
    return (
        antiherm
        - diagonal_mask(0) * trace_re[..., None, :] / 3.0
        - diagonal_mask(1) * trace_im[..., None, :] / 3.0
    )


def expmap(generator):
    unit_matrix = diagonal_mask(0)
    result = unit_matrix + generator / 8.0
    for degree in range(7, 0, -1):
        result = unit_matrix + multiply(generator, result) / float(degree)
    return result


def shifted(values, step_y, step_x):
    if step_y != 0:
        values = jnp.roll(values, -step_y * X, axis=-1)
    if step_x != 0:
        column = jnp.arange(values.shape[-1]) % X
        if step_x == 1:
            values = jnp.where(
                column == X - 1, jnp.roll(values, X - 1, axis=-1), jnp.roll(values, -1, axis=-1)
            )
        else:
            values = jnp.where(
                column == 0, jnp.roll(values, 1 - X, axis=-1), jnp.roll(values, 1, axis=-1)
            )
    return values


def unit_step(direction):
    return tuple((1 if position == direction else 0 for position in range(4)))


def combine(first, second, factor):
    return tuple((first[position] + factor * second[position] for position in range(4)))


def fetch_link(padded, direction, offset):
    inner_t = padded.shape[0] - 2
    inner_z = padded.shape[1] - 2
    window = padded[
        1 + offset[0] : 1 + offset[0] + inner_t, 1 + offset[1] : 1 + offset[1] + inner_z, direction
    ]
    return shifted(window, offset[2], offset[3])


def forces(padded):
    anchor = (0, 0, 0, 0)
    drifts = []
    for forward in range(4):
        forward_step = unit_step(forward)
        total_sum = None
        for sideways in range(4):
            if sideways == forward:
                continue
            across = unit_step(sideways)
            beneath = combine(anchor, across, -1)
            behind = combine(forward_step, across, -1)
            upper_loop = multiply(
                multiply(
                    fetch_link(padded, sideways, forward_step),
                    dagger(fetch_link(padded, forward, across)),
                ),
                dagger(fetch_link(padded, sideways, anchor)),
            )
            lower_loop = multiply(
                multiply(
                    dagger(fetch_link(padded, sideways, behind)),
                    dagger(fetch_link(padded, forward, beneath)),
                ),
                fetch_link(padded, sideways, beneath),
            )
            staple = upper_loop + lower_loop
            total_sum = staple if total_sum is None else total_sum + staple
        loop_sum = multiply(fetch_link(padded, forward, anchor), total_sum)
        drifts.append(-flow_step * project(loop_sum))
    return jnp.stack(drifts, axis=2)


def gather_rims(lattice):
    extended = with_halo(lattice, (("gz", 1),), 1)
    return with_halo(extended, (("ta", 0),), 1)


def shards(links):
    full_shape = links.shape
    lattice = links.reshape(full_shape[0], full_shape[1], 4, 18, full_shape[3])
    drift_first = forces(gather_rims(lattice))
    section_one = multiply(expmap(0.25 * drift_first), lattice)
    drift_second = forces(gather_rims(section_one))
    result = multiply(expmap(8.0 / 9.0 * drift_second - 17.0 / 36.0 * drift_first), section_one)
    return result.reshape(full_shape)


def solution(mesh):
    in_specs = (P(("cfg", "ta"), "gz", None, None),)
    out_specs = P(("cfg", "ta"), "gz", None, None)
    return jax.shard_map(shards, mesh=mesh, in_specs=in_specs, out_specs=out_specs, check_vma=False)
```

profile of v0, /device:TPU:0, one launch (start us, length us, event | category | flops | bytes accessed | tf_op | source)
XLA Modules:
  0.0 506.7 jit_solution(14252570768264042763)
XLA Ops:
  0.0 1.8 reshape.141364
  7.6 1.2 broadcast_select_fusion.25
  13.1 1.2 broadcast_select_fusion.9
  15.1 1.9 pad_maximum_fusion
  17.0 6.0 %collective-permute-start.2 = (f32[1,3,4,18,2304]{4,0,3,2,1:T(1,128)S(1)}, f32[1,3,4,18,2304]{4,0,3,2,1:T(1,128)S(1)}, u32[]{:S(2)}, u32[]{:S(2)}) collective-permute-start(f32[1,3,4,18,2304]{4,0,3,2,1:T(1,128)S(1)} %pad_maximum_fusion), channel_id=1, source_target_pairs={{2,0},{4,2},{6,4},{8,6},{10,8},{12,10},{14,12},{0,14},{3,1},{5,3},... | collective-permute-start | bytes 5971976 | tf_op jit(solution)/shard_map/ppermute | solution.py:21
  34.3 71.9 %collective-permute-done.2 = f32[1,3,4,18,2304]{4,0,3,2,1:T(1,128)S(1)} collective-permute-done((f32[1,3,4,18,2304]{4,0,3,2,1:T(1,128)S(1)}, f32[1,3,4,18,2304]{4,0,3,2,1:T(1,128)S(1)}, u32[]{:S(2)}, u32[]{:S(2)}) %collective-permute-start.2) | collective-permute-done | bytes 1990688 | tf_op jit(solution)/shard_map/ppermute | solution.py:21
  109.0 2.5 broadcast_select_fusion.13
  123.6 2.7 broadcast_select_fusion.22
  157.7 1.7 multiply_bitcast_fusion.7
  172.5 1.3 multiply_add_fusion.12
  186.1 1.3 multiply_add_fusion.11
  199.7 1.3 multiply_add_fusion.10
  205.1 1.2 constant_dynamic-update-slice_fusion.785
  213.8 1.3 multiply_add_fusion.9
  227.4 1.3 multiply_add_fusion.8
  241.0 1.3 multiply_add_fusion.7
  254.6 1.3 broadcast_add_fusion
  264.7 1.3 broadcast_select_fusion.2
  267.5 4.7 collective-permute-start.6
  283.6 1.1 broadcast_select_fusion.15
  290.5 62.7 %collective-permute-done.7 = f32[1,3,4,18,2304]{4,0,3,2,1:T(1,128)S(1)} collective-permute-done((f32[1,3,4,18,2304]{4,0,3,2,1:T(1,128)S(1)}, f32[1,3,4,18,2304]{4,0,3,2,1:T(1,128)S(1)}, u32[]{:S(2)}, u32[]{:S(2)}) %collective-permute-start.7) | collective-permute-done | bytes 1990688 | tf_op jit(solution)/shard_map/ppermute | solution.py:18
  353.8 2.8 collective-permute-done.6
  357.8 2.3 broadcast_select_fusion.16
  361.8 2.7 broadcast_select_fusion.6
  406.1 1.7 multiply_bitcast_fusion.3
  421.9 1.3 multiply_add_fusion.5
  435.3 1.3 multiply_add_fusion.4
  448.7 1.3 multiply_add_fusion.3
  462.2 1.3 multiply_add_fusion.2
  475.7 1.3 multiply_add_fusion.1
  489.1 1.3 multiply_add_fusion
  502.5 1.3 broadcast_add_fusion.1
  (1817 shorter events, 313.9 us)
Async XLA Ops:
  1.8 12.7 %collective-permute-start.1 = (f32[1,1,4,18,2304]{4,0,3,2,1:T(1,128)S(1)}, f32[1,1,4,18,2304]{4,0,3,2,1:T(1,128)S(1)}, u32[]{:S(2)}, u32[]{:S(2)}) collective-permute-start(f32[1,1,4,18,2304]{4,0,3,2,1:T(1,128)S(1)} %bitcast.744), channel_id=1, source_target_pairs={{1,0},{0,1},{3,2},{2,3},{5,4},{4,5},{7,6},{6,7},{9,8},{8,9},{11,10... | collective-permute-start | bytes 1990664 | tf_op jit(solution)/shard_map/ppermute | solution.py:21
  2.3 12.8 %collective-permute-start = (f32[1,1,4,18,2304]{4,0,3,2,1:T(1,128)S(1)}, f32[1,1,4,18,2304]{4,0,3,2,1:T(1,128)S(1)}, u32[]{:S(2)}, u32[]{:S(2)}) collective-permute-start(f32[1,1,4,18,2304]{4,0,3,2,1:T(1,128)S(1)} %bitcast.745), channel_id=1, source_target_pairs={{0,1},{1,0},{2,3},{3,2},{4,5},{5,4},{6,7},{7,6},{8,9},{9,8},{10,11... | collective-permute-start | bytes 1990664 | tf_op jit(solution)/shard_map/ppermute | solution.py:18
  17.0 89.2 %collective-permute-start.2 = (f32[1,3,4,18,2304]{4,0,3,2,1:T(1,128)S(1)}, f32[1,3,4,18,2304]{4,0,3,2,1:T(1,128)S(1)}, u32[]{:S(2)}, u32[]{:S(2)}) collective-permute-start(f32[1,3,4,18,2304]{4,0,3,2,1:T(1,128)S(1)} %pad_maximum_fusion), channel_id=1, source_target_pairs={{2,0},{4,2},{6,4},{8,6},{10,8},{12,10},{14,12},{0,14},{3,1},{5,3},... | collective-permute-start | bytes 5971976 | tf_op jit(solution)/shard_map/ppermute | solution.py:21
  23.0 99.8 %collective-permute-start.3 = (f32[1,3,4,18,2304]{4,0,3,2,1:T(1,128)S(1)}, f32[1,3,4,18,2304]{4,0,3,2,1:T(1,128)S(1)}, u32[]{:S(2)}, u32[]{:S(2)}) collective-permute-start(f32[1,3,4,18,2304]{4,0,3,2,1:T(1,128)S(1)} %pad_maximum_fusion), channel_id=1, source_target_pairs={{0,2},{2,4},{4,6},{6,8},{8,10},{10,12},{12,14},{14,0},{1,3},{3,5},... | collective-permute-start | bytes 5971976 | tf_op jit(solution)/shard_map/ppermute | solution.py:18
  155.4 2.3 copy-start
  155.4 2.3 copy-start.1
  258.4 8.1 %collective-permute-start.4 = (f32[1,1,4,18,2304]{4,0,3,2,1:T(1,128)S(1)}, f32[1,1,4,18,2304]{4,0,3,2,1:T(1,128)S(1)}, u32[]{:S(2)}, u32[]{:S(2)}) collective-permute-start(f32[1,1,4,18,2304]{4,0,3,2,1:T(1,128)S(1)} %copy.53), channel_id=1, source_target_pairs={{0,1},{1,0},{2,3},{3,2},{4,5},{5,4},{6,7},{7,6},{8,9},{9,8},{10,11... | collective-permute-start | bytes 1990664 | tf_op jit(solution)/shard_map/ppermute | solution.py:18
  258.4 8.8 %collective-permute-start.5 = (f32[1,1,4,18,2304]{4,0,3,2,1:T(1,128)S(1)}, f32[1,1,4,18,2304]{4,0,3,2,1:T(1,128)S(1)}, u32[]{:S(2)}, u32[]{:S(2)}) collective-permute-start(f32[1,1,4,18,2304]{4,0,3,2,1:T(1,128)S(1)} %copy.53), channel_id=1, source_target_pairs={{1,0},{0,1},{3,2},{2,3},{5,4},{4,5},{7,6},{6,7},{9,8},{8,9},{11,10... | collective-permute-start | bytes 1990664 | tf_op jit(solution)/shard_map/ppermute | solution.py:21
  267.4 85.8 %collective-permute-start.7 = (f32[1,3,4,18,2304]{4,0,3,2,1:T(1,128)S(1)}, f32[1,3,4,18,2304]{4,0,3,2,1:T(1,128)S(1)}, u32[]{:S(2)}, u32[]{:S(2)}) collective-permute-start(f32[1,3,4,18,2304]{4,0,3,2,1:T(1,128)S(1)} %constant_dynamic-update-slice_fusion.864), channel_id=1, source_target_pairs={{0,2},{2,4},{4,6},{6,8},{8,10},{10,12},{12,14},{14,0},{1,3},{3,5},... | collective-permute-start | bytes 5971976 | tf_op jit(solution)/shard_map/ppermute | solution.py:18
  267.5 89.2 %collective-permute-start.6 = (f32[1,3,4,18,2304]{4,0,3,2,1:T(1,128)S(1)}, f32[1,3,4,18,2304]{4,0,3,2,1:T(1,128)S(1)}, u32[]{:S(2)}, u32[]{:S(2)}) collective-permute-start(f32[1,3,4,18,2304]{4,0,3,2,1:T(1,128)S(1)} %constant_dynamic-update-slice_fusion.864), channel_id=1, source_target_pairs={{2,0},{4,2},{6,4},{8,6},{10,8},{12,10},{14,12},{0,14},{3,1},{5,3},... | collective-permute-start | bytes 5971976 | tf_op jit(solution)/shard_map/ppermute | solution.py:21
where the time goes:
time: 516 us; the launch traced here: 507 us
  other arithmetic  329 us (64%)
  waiting for transfers between devices  137 us (27%)
  local copies, waits for them, and re-layouts  24.8 us (5%)
  starting transfers between devices  12.4 us (2%)
    unnamed x1288, other arithmetic  264 us
    ppermute x4, waiting for transfers between devices, with_halo(): lax.ppermute(lax.slice_in_dim(block, 0, width, axis=dim), axis, backward)  74.7 us
    ppermute x4, waiting for transfers between devices, with_halo(): lax.ppermute(lax.slice_in_dim(block, block.shape[dim] - width, None, axis...  62.7 us
    add x14, other arithmetic, expmap(): result = unit_matrix + multiply(generator, result) / float(degree)  18 us
    another operation x64, other arithmetic, multiply(): return jnp.stack(entries, axis=-2)  13.5 us
    ppermute x4, starting transfers between devices, with_halo(): lax.ppermute(lax.slice_in_dim(block, 0, width, axis=dim), axis, backward)  11.8 us
  transfers between devices with their start and end apart: 8, of which 3 were waited for; matrix products, arithmetic and copies ran while one was open for 13% of the time, Pallas kernels for 0%

commit v1 on v0

v1 whole, which is shorter than its diff:
```python
import jax
import jax.numpy as jnp
from jax import lax
from jax.experimental import pallas as pl
from jax.experimental.pallas import tpu as pltpu
from jax.sharding import PartitionSpec as P

X = 48
ROWS = 18
LANES = 128
PAD = 24
BASE = 8
HALO = 32
flow_step = 0.05


def dot3(lefts, rights, conj_left, conj_right, want=(True, True)):
    real = imag = None
    for (ar, ai), (br, bi) in zip(lefts, rights):
        if want[0]:
            first = ar * br
            second = ai * bi
            term = first + second if conj_left != conj_right else first - second
            real = term if real is None else real + term
        if want[1]:
            first = ar * bi
            second = ai * br
            if conj_left and conj_right:
                term = -(first + second)
            elif conj_left:
                term = first - second
            elif conj_right:
                term = second - first
            else:
                term = first + second
            imag = term if imag is None else imag + term
    return real, imag


def product(a, b, adj_a=False, adj_b=False, rows=3):
    out = []
    for i in range(rows):
        left = [a[k][i] if adj_a else a[i][k] for k in range(3)]
        out.append(
            [
                dot3(left, [b[j][k] if adj_b else b[k][j] for k in range(3)], adj_a, adj_b)
                for j in range(3)
            ]
        )
    return out


def antiherm_product(a, b, adj_b=False):
    def entry(i, j, want=(True, True)):
        return dot3(
            [a[i][k] for k in range(3)],
            [b[j][k] if adj_b else b[k][j] for k in range(3)],
            False,
            adj_b,
            want,
        )

    out = []
    for i in range(3):
        value = entry(i, i, (False, True))[1]
        out.append(value + value)
    for i, j in ((0, 1), (0, 2), (1, 2)):
        up = entry(i, j)
        low = entry(j, i)
        out.append(up[0] - low[0])
        out.append(up[1] + low[1])
    return out


def third_row(rows):
    a, b = rows
    out = []
    for j in range(3):
        k, m = (j + 1) % 3, (j + 2) % 3
        (pr, pi), (qr, qi) = a[k], b[m]
        (sr, si), (tr, ti) = a[m], b[k]
        out.append(
            ((pr * qr - pi * qi) - (sr * tr - si * ti), (sr * ti + si * tr) - (pr * qi + pi * qr))
        )
    return out


def expmap(q):
    d = q[:3]
    h = [(q[4], -q[3]), (q[6], -q[5]), (q[8], -q[7])]
    n = [r * r + i * i for r, i in h]
    s = [
        d[0] * d[0] + n[0] + n[1],
        d[1] * d[1] + n[0] + n[2],
        d[2] * d[2] + n[1] + n[2],
    ]
    (ar, ai), (br, bi), (cr, ci) = h
    e01 = d[0] + d[1]
    e02 = d[0] + d[2]
    e12 = d[1] + d[2]
    w_r = ar * cr - ai * ci
    w_i = ar * ci + ai * cr
    so = [
        (e01 * ar + (br * cr + bi * ci), e01 * ai + (bi * cr - br * ci)),
        (e02 * br + w_r, e02 * bi + w_i),
        (e12 * cr + (ar * br + ai * bi), e12 * ci + (ar * bi - ai * br)),
    ]
    p = 0.5 * (s[0] + s[1] + s[2])
    det = (
        d[0] * d[1] * d[2]
        + 2.0 * (w_r * br + w_i * bi)
        - d[0] * n[2]
        - d[1] * n[1]
        - d[2] * n[0]
    )
    dd = det * det
    pp = p * p
    top = dd + pp * p
    f0r = 1.0 - dd * (1.0 / 720.0 - p * (2.0 / 40320.0))
    f1r = det * (1.0 / 24.0 - p * (2.0 / 720.0) + pp * (3.0 / 40320.0))
    f2r = -0.5 + p * (1.0 / 24.0) - pp * (1.0 / 720.0) + top * (1.0 / 40320.0)
    f0i = det * (-1.0 / 6.0 + p * (1.0 / 120.0) - pp * (1.0 / 5040.0))
    f1i = 1.0 - p * (1.0 / 6.0) + pp * (1.0 / 120.0) - top * (1.0 / 5040.0)
    f2i = det * (1.0 / 120.0 - p * (2.0 / 5040.0))
    out = [[None] * 3 for _ in range(3)]
    for i in range(3):
        out[i][i] = (f0r + f1r * d[i] + f2r * s[i], f0i + f1i * d[i] + f2i * s[i])
    for (i, j), (hr, hi), (sr, si) in zip(((0, 1), (0, 2), (1, 2)), h, so):
        rr = f1r * hr + f2r * sr
        ii = f1i * hi + f2i * si
        ri = f1r * hi + f2r * si
        ir = f1i * hr + f2i * sr
        out[i][j] = (rr - ii, ri + ir)
        out[j][i] = (rr + ii, ir - ri)
    return out


def load(ref, mat, rows, count=3):
    return [
        [
            (ref[mat * 18 + (i * 3 + j) * 2, rows, :], ref[mat * 18 + (i * 3 + j) * 2 + 1, rows, :])
            for j in range(3)
        ]
        for i in range(count)
    ]


def store(ref, base, rows, matrix):
    for i, row in enumerate(matrix):
        for j, (re, im) in enumerate(row):
            ref[base + (i * 3 + j) * 2, rows, :] = re
            ref[base + (i * 3 + j) * 2 + 1, rows, :] = im


def wrap_rows(ref):
    ref[:, BASE - 1 : BASE, :] = ref[:, BASE + ROWS - 1 : BASE + ROWS, :]
    ref[:, BASE + ROWS : BASE + ROWS + 1, :] = ref[:, BASE : BASE + 1, :]


def shift_value(here, after, before, step, lane, column):
    if step == "+y":
        return pltpu.roll(jnp.where(lane >= X, here, after), LANES - X, 1)
    if step == "-y":
        return pltpu.roll(jnp.where(lane < LANES - X, here, before), X, 1)
    if step == "+x":
        near = pltpu.roll(jnp.where(lane >= 1, here, after), LANES - 1, 1)
        far = pltpu.roll(jnp.where(lane < LANES - X + 1, here, before), X - 1, 1)
        return jnp.where(column == X - 1, far, near)
    near = pltpu.roll(jnp.where(lane < LANES - 1, here, before), 1, 1)
    far = pltpu.roll(jnp.where(lane >= X - 1, here, after), LANES - X + 1, 1)
    return jnp.where(column == 0, far, near)


def shift_matrices(source, source_mat, target, target_mat, count, step):
    lane = lax.broadcasted_iota(jnp.int32, (ROWS, LANES), 1)
    row = lax.broadcasted_iota(jnp.int32, (ROWS, LANES), 0)
    column = lax.rem(row * LANES + lane, X)

    def body(group, carry):
        for inner in range(6):
            index = group * 6 + inner
            here = source[source_mat * 18 + index, BASE : BASE + ROWS, :]
            after = source[source_mat * 18 + index, BASE + 1 : BASE + ROWS + 1, :]
            before = source[source_mat * 18 + index, BASE - 1 : BASE + ROWS - 1, :]
            target[target_mat * 18 + index, 0:ROWS, :] = shift_value(
                here, after, before, step, lane, column
            )
        return carry

    lax.fori_loop(0, count * 3, body, 0)


def pack_kernel(u_ref, out_ref):
    for d in range(3):
        out_ref[:, d * ROWS : (d + 1) * ROWS, :] = u_ref[(d + 1) * 18 : (d + 1) * 18 + 12, 0:ROWS, :]


def transport_kernel(u_ref, b_ref, out_ref, field, moved, scr):
    field[:, BASE : BASE + ROWS, :] = u_ref[0:18, 0:ROWS, :]
    wrap_rows(field)
    shift_matrices(field, 0, moved, 0, 1, "+y")
    shift_matrices(field, 0, moved, 1, 1, "+x")

    def body(chunk, carry):
        rows = pl.ds(pl.multiple_of(chunk * 8, 8), 8)
        time_link = load(u_ref, 0, rows)
        for d in range(3):
            ahead = load(b_ref, 0, rows) if d == 0 else load(moved, d - 1, rows)
            right = product(load(u_ref, d + 1, rows), ahead)
            store(scr, d * 12, rows, product(time_link, right, adj_a=True, rows=2))
        return carry

    lax.fori_loop(0, 3, body, 0)
    for d in range(3):
        out_ref[:, d * ROWS : (d + 1) * ROWS, :] = scr[d * 12 : d * 12 + 12, 0:ROWS, :]


def unpack(ref, source_row, target, mat):
    for e in range(12):
        target[mat * 18 + e, 0:ROWS, :] = ref[e, source_row : source_row + ROWS, :]


def rebuild(target, mats, rows):
    for mat in mats:
        last = third_row(load(target, mat, rows, 2))
        store(target, mat * 18 + 12, rows, [last])


def section_kernel(
    second, u_ref, b_ref, t_ref, w_ref, c_ref, *rest
):
    if second:
        d_ref, out_ref = rest[:2]
        rest = rest[2:]
    else:
        out_ref, drift_ref, pack_ref = rest[:3]
        rest = rest[3:]
    field, sib, fx, fy, halo, low, lowm, force = rest
    field[:, BASE : BASE + ROWS, :] = u_ref[:, 0:ROWS, :]
    wrap_rows(field)
    sib[:, BASE : BASE + ROWS, :] = b_ref[18:36, 0:ROWS, :]
    wrap_rows(sib)
    for d in range(3):
        unpack(t_ref, d * ROWS, halo, d)
        unpack(w_ref, d * ROWS, halo, 3 + d)
    unpack(c_ref, 0, halo, 6)
    shift_matrices(field, 0, fx, 0, 3, "+x")
    shift_matrices(sib, 0, fx, 3, 1, "+x")
    shift_matrices(field, 0, fy, 0, 2, "+y")
    shift_matrices(field, 3, fy, 2, 1, "+y")
    shift_matrices(sib, 0, fy, 3, 1, "+y")

    def planes(chunk, carry):
        rows = pl.ds(pl.multiple_of(chunk * 8, 8), 8)
        inner = pl.ds(pl.multiple_of(chunk * 8 + BASE, 8), 8)
        rebuild(halo, range(7), rows)

        def link(mu, nu):
            if nu == 0:
                return load(halo, mu - 1, rows)
            if nu == 1:
                return load(b_ref, mu, rows)
            if nu == 2:
                return load(fy, {0: 0, 1: 1, 3: 2}[mu], rows)
            return load(fx, mu, rows)

        totals = [None] * 4
        for mu, nu in ((0, 1), (0, 2), (0, 3), (1, 2), (1, 3), (2, 3)):
            first = load(u_ref, mu, rows)
            other = load(u_ref, nu, rows)
            near = product(first, link(nu, mu))
            far = product(other, link(mu, nu))
            loop = antiherm_product(near, far, adj_b=True)
            if totals[mu] is None:
                totals[mu] = loop
            else:
                totals[mu] = [a + b for a, b in zip(totals[mu], loop)]
            if totals[nu] is None:
                totals[nu] = [-b for b in loop]
            else:
                totals[nu] = [a - b for a, b in zip(totals[nu], loop)]
            if nu == 2:
                store(low, (3 + mu) * 18, inner, product(near, other, adj_a=True))
            if nu == 3:
                store(low, mu * 18, inner, product(near, other, adj_a=True))
            if (mu, nu) == (2, 3):
                store(low, 5 * 18, inner, product(far, first, adj_a=True))
        for mu in range(4):
            for k in range(9):
                force[mu * 9 + k, rows, :] = totals[mu][k]
        return carry

    lax.fori_loop(0, 3, planes, 0)
    wrap_rows(low)
    shift_matrices(low, 0, lowm, 0, 3, "-x")
    shift_matrices(low, 3, lowm, 3, 3, "-y")

    def finish(chunk, carry):
        rows = pl.ds(pl.multiple_of(chunk * 8, 8), 8)
        for mu in range(4):
            parts = []
            if mu != 1:
                ahead = (
                    load(halo, 6, rows)
                    if mu == 0
                    else load(fy, 3, rows)
                    if mu == 2
                    else load(fx, 3, rows)
                )
                inner = product(load(b_ref, mu, rows), load(b_ref, 1, rows), adj_a=True)
                parts.append(product(ahead, inner, adj_a=True))
            if mu != 3:
                parts.append(load(lowm, mu, rows))
            if mu != 2:
                parts.append(load(lowm, {0: 3, 1: 4, 3: 5}[mu], rows))
            total = parts[0]
            for part in parts[1:]:
                total = [
                    [(a[0] + b[0], a[1] + b[1]) for a, b in zip(ra, rb)]
                    for ra, rb in zip(total, part)
                ]
            if mu != 0:
                moved = load(halo, 2 + mu, rows)
                total = [
                    [
                        (total[i][j][0] + moved[j][i][0], total[i][j][1] - moved[j][i][1])
                        for j in range(3)
                    ]
                    for i in range(3)
                ]
            own = load(u_ref, mu, rows)
            loop = antiherm_product(own, total)
            loop = [loop[k] + force[mu * 9 + k, rows, :] for k in range(9)]
            mean = (loop[0] + loop[1] + loop[2]) * (1.0 / 3.0)
            loop = [loop[k] - mean if k < 3 else loop[k] for k in range(9)]
            if second:
                generator = [
                    loop[k] * (-0.5 * flow_step * 8.0 / 9.0)
                    - (17.0 / 36.0) * d_ref[mu * 9 + k, rows, :]
                    for k in range(9)
                ]
            else:
                drift = [value * (-0.5 * flow_step) for value in loop]
                for k in range(9):
                    drift_ref[mu * 9 + k, rows, :] = drift[k]
                generator = [0.25 * value for value in drift]
            store(out_ref, mu * 18, rows, product(expmap(generator), own))
        return carry

    lax.fori_loop(0, 3, finish, 0)
    if not second:
        pack_kernel(out_ref, pack_ref)


VM = pl.BlockSpec(memory_space=pltpu.VMEM)


def f32(*shape):
    return jax.ShapeDtypeStruct(shape, jnp.float32)


def call(kernel, outs, inputs, scratch):
    return pl.pallas_call(
        kernel,
        out_shape=outs,
        in_specs=[VM] * len(inputs),
        out_specs=jax.tree.map(lambda _: VM, outs),
        scratch_shapes=[pltpu.VMEM(shape, jnp.float32) for shape in scratch],
        compiler_params=pltpu.CompilerParams(vmem_limit_bytes=40 * 2**20),
    )(*inputs)


def section(links, pack, drift):
    count = lax.axis_size("ta")
    forward = [(i, (i + 1) % count) for i in range(count)]
    backward = [(target, source) for source, target in forward]
    swap = [(0, 1), (1, 0)]
    sibling = lax.ppermute(links, "gz", swap)
    ahead = lax.ppermute(pack, "ta", backward)
    transported = call(
        transport_kernel,
        f32(12, 3 * ROWS, LANES),
        [links, sibling],
        [(18, HALO, LANES), (36, PAD, LANES), (36, PAD, LANES)],
    )
    behind = lax.ppermute(transported, "ta", forward)
    corner = lax.ppermute(ahead[:, :ROWS], "gz", swap)
    inputs = [links, sibling, ahead, behind, corner]
    scratch = [
        (72, HALO, LANES),
        (18, HALO, LANES),
        (72, PAD, LANES),
        (72, PAD, LANES),
        (126, PAD, LANES),
        (108, HALO, LANES),
        (108, PAD, LANES),
        (36, PAD, LANES),
    ]
    if drift is None:
        outs = [f32(72, PAD, LANES), f32(36, PAD, LANES), f32(12, 3 * ROWS, LANES)]
        kernel = lambda *refs: section_kernel(False, *refs)
    else:
        outs = f32(72, PAD, LANES)
        inputs.append(drift)
        kernel = lambda *refs: section_kernel(True, *refs)
    return call(kernel, outs, inputs, scratch)


def shards(links):
    full_shape = links.shape
    first = jnp.pad(links.reshape(72, ROWS, LANES), ((0, 0), (0, PAD - ROWS), (0, 0)))
    pack = call(pack_kernel, f32(12, 3 * ROWS, LANES), [first], [])
    middle, drift, pack = section(first, pack, None)
    result = section(middle, pack, drift)
    return result[:, :ROWS].reshape(full_shape)


def solution(mesh):
    in_specs = (P(("cfg", "ta"), "gz", None, None),)
    out_specs = P(("cfg", "ta"), "gz", None, None)
    return jax.shard_map(shards, mesh=mesh, in_specs=in_specs, out_specs=out_specs, check_vma=False)
```

time: 516 us -> 59.7 us (0.12); the launches traced: 507 us -> 58.8 us
  other arithmetic: 329 us -> 0 us
  waiting for transfers between devices: 137 us -> 25.5 us
  local copies, waits for them, and re-layouts: 24.8 us -> 2.21 us
  Pallas kernels: 0 us -> 17.9 us
    unnamed x1288 -> x0, other arithmetic: 264 us -> none
    ppermute x8, waiting for transfers between devices: 137 us -> 25.5 us  [the longest x2 13.7 us: section(): ahead = lax.ppermute(pack, 'ta', backward)]
    add x31 -> x0, other arithmetic: 22.6 us -> none  [the longest x14 18 us: expmap(): result = unit_matrix + multiply(generator, result) / float(degree)]
    pallas_call x0 -> x5, Pallas kernels: none -> 17.9 us  [call(): pl.pallas_call(kernel, out_shape=outs, in_specs=[VM] * len(inputs), out_s...]
    another operation x82 -> x0, other arithmetic: 17.9 us -> none  [the longest x64 13.5 us: multiply(): return jnp.stack(entries, axis=-2)]
    slice x73 -> x2, local copies, waits for them, and re-layouts: 15.8 us -> 0.02 us  [section(): corner = lax.ppermute(ahead[:, :ROWS], 'gz', swap)]
    select_n x8 -> x0, other arithmetic: 14.9 us -> none  [the longest x4 7.65 us: shifted(): jnp.where(column == 0, jnp.roll(values, 1 - X, axis=-1), jnp.roll(values,...]
    concatenate x21 -> x0, other arithmetic: 6.22 us -> none  [the longest x20 4.32 us: shifted(): values = jnp.roll(values, -step_y * X, axis=-1)]
  transfers between devices with their start and end apart: 8 -> 8, of which waited for: 3 -> 6; matrix products, arithmetic and copies ran while one was open for 13% -> 0% of each run, Pallas kernels for 0% -> 4%
where the time goes in v1:
time: 59.7 us; the launch traced here: 58.8 us
  waiting for transfers between devices  25.5 us (43%)
  Pallas kernels  17.9 us (30%)
  starting transfers between devices  13.1 us (22%)
  local copies, waits for them, and re-layouts  2.21 us (4%)
    pallas_call x5, Pallas kernels, call(): pl.pallas_call(kernel, out_shape=outs, in_specs=[VM] * len(inputs), out_s...  17.9 us
    ppermute x2, waiting for transfers between devices, section(): ahead = lax.ppermute(pack, 'ta', backward)  13.7 us
    ppermute x2, starting transfers between devices, section(): ahead = lax.ppermute(pack, 'ta', backward)  12.2 us
    ppermute x2, waiting for transfers between devices, section(): behind = lax.ppermute(transported, 'ta', forward)  9.11 us
    ppermute x2, waiting for transfers between devices, section(): corner = lax.ppermute(ahead[:, :ROWS], 'gz', swap)  2.72 us
  transfers between devices with their start and end apart: 8, of which 6 were waited for; matrix products, arithmetic and copies ran while one was open for 0% of the time, Pallas kernels for 4%

profile of v1, /device:TPU:0, one launch (start us, length us, event | category | flops | bytes accessed | tf_op | source)
XLA Modules:
  0.0 58.8 jit_solution(2207105630910806373)
XLA Ops:
  0.0 1.2 %reshape.6 = f32[72,18,128]{2,1,0:T(8,128)S(1)} reshape(f32[1,1,72,2304]{3,2,1,0:T(8,128)} %param.1) | data formatting | bytes 1327104 | tf_op jit(solution)/shard_map/reshape | solution.py:411
  1.2 0.1 pad.4.u_ref.refs_0_
  1.3 0.5 collective-permute-start
  1.8 5.6 %collective-permute-start.1 = (f32[12,54,128]{2,1,0:T(8,128)S(1)}, f32[12,54,128]{2,1,0:T(8,128)S(1)}, u32[]{:S(2)}, u32[]{:S(2)}) collective-permute-start(f32[12,54,128]{2,1,0:T(8,128)S(1)} %shard_map.17), channel_id=1, source_target_pairs={{2,0},{4,2},{6,4},{8,6},{10,8},{12,10},{14,12},{0,14},{3,1},{5,3},... | collective-permute-start | bytes 995336 | tf_op jit(solution)/shard_map/ppermute | solution.py:379
  7.4 0.0 collective-permute-done.b_ref.refs_1_
  7.4 1.0 %shard_map.18 = f32[12,54,128]{2,1,0:T(8,128)S(1)} custom-call(f32[72,24,128]{2,1,0:T(8,128)S(1)} %pad.4.u_ref.refs_0_, f32[72,24,128]{2,1,0:T(8,128)S(1)} %collective-permute-done.b_ref.refs_1_), custom_call_target="tpu_custom_call" | custom-call | tf_op jit(solution)/shard_map/pallas_call | solution.py:363
  8.5 0.1 collective-permute-start.2
  8.6 6.9 %collective-permute-done.1.refs_2_ = f32[12,54,128]{2,1,0:T(8,128)S(1)} collective-permute-done((f32[12,54,128]{2,1,0:T(8,128)S(1)}, f32[12,54,128]{2,1,0:T(8,128)S(1)}, u32[]{:S(2)}, u32[]{:S(2)}) %collective-permute-start.1) | collective-permute-done | bytes 331808 | tf_op jit(solution)/shard_map/ppermute | solution.py:379
  15.4 0.1 collective-permute-start.3
  15.5 1.4 %collective-permute-done.3.refs_4_ = f32[12,18,128]{2,1,0:T(8,128)S(1)} collective-permute-done((f32[12,18,128]{2,1,0:T(8,128)S(1)}, f32[12,18,128]{2,1,0:T(8,128)S(1)}, u32[]{:S(2)}, u32[]{:S(2)}) %collective-permute-start.3) | collective-permute-done | bytes 110624 | tf_op jit(solution)/shard_map/ppermute | solution.py:387
  16.9 4.6 %collective-permute-done.2.refs_3_ = f32[12,54,128]{2,1,0:T(8,128)S(1)} collective-permute-done((f32[12,54,128]{2,1,0:T(8,128)S(1)}, f32[12,54,128]{2,1,0:T(8,128)S(1)}, u32[]{:S(2)}, u32[]{:S(2)}) %collective-permute-start.2) | collective-permute-done | bytes 331808 | tf_op jit(solution)/shard_map/ppermute | solution.py:386
  21.4 7.9 %shard_map.19 = (f32[72,24,128]{2,1,0:T(8,128)S(1)}, f32[36,24,128]{2,1,0:T(8,128)S(1)}, f32[12,54,128]{2,1,0:T(8,128)S(1)}) custom-call(f32[72,24,128]{2,1,0:T(8,128)S(1)} %pad.4.u_ref.refs_0_, f32[72,24,128]{2,1,0:T(8,128)S(1)} %collective-permute-done.b_ref.refs_1_, f32[12,54,128]{2,1,0:T(8,128)S(1)} %collective-permute-done.1.refs_2_, ...), custom_call_target="tpu_custom_call" | custom-call | tf_op jit(solution)/shard_map/pallas_call | solution.py:363
  29.3 0.1 collective-permute-start.4
  29.4 6.6 %collective-permute-start.5 = (f32[12,54,128]{2,1,0:T(8,128)S(1)}, f32[12,54,128]{2,1,0:T(8,128)S(1)}, u32[]{:S(2)}, u32[]{:S(2)}) collective-permute-start(f32[12,54,128]{2,1,0:T(8,128)S(1)} %get-tuple-element.9), channel_id=1, source_target_pairs={{2,0},{4,2},{6,4},{8,6},{10,8},{12,10},{14,12},{0,14},{3,1},{5,3},... | collective-permute-start | bytes 995336 | tf_op jit(solution)/shard_map/ppermute | solution.py:379
  36.0 0.0 collective-permute-done.4.b_ref.refs_1_
  36.0 1.0 %shard_map.20 = f32[12,54,128]{2,1,0:T(8,128)S(1)} custom-call(f32[72,24,128]{2,1,0:T(8,128)S(1)} %get-tuple-element.8.u_ref.refs_0_, f32[72,24,128]{2,1,0:T(8,128)S(1)} %collective-permute-done.4.b_ref.refs_1_), custom_call_target="tpu_custom_call" | custom-call | tf_op jit(solution)/shard_map/pallas_call | solution.py:363
  37.1 0.1 collective-permute-start.6
  37.1 6.8 %collective-permute-done.5.refs_2_ = f32[12,54,128]{2,1,0:T(8,128)S(1)} collective-permute-done((f32[12,54,128]{2,1,0:T(8,128)S(1)}, f32[12,54,128]{2,1,0:T(8,128)S(1)}, u32[]{:S(2)}, u32[]{:S(2)}) %collective-permute-start.5) | collective-permute-done | bytes 331808 | tf_op jit(solution)/shard_map/ppermute | solution.py:379
  43.9 0.1 collective-permute-start.7
  44.0 1.4 %collective-permute-done.7.refs_4_ = f32[12,18,128]{2,1,0:T(8,128)S(1)} collective-permute-done((f32[12,18,128]{2,1,0:T(8,128)S(1)}, f32[12,18,128]{2,1,0:T(8,128)S(1)}, u32[]{:S(2)}, u32[]{:S(2)}) %collective-permute-start.7) | collective-permute-done | bytes 110624 | tf_op jit(solution)/shard_map/ppermute | solution.py:387
  45.4 4.6 %collective-permute-done.6.refs_3_ = f32[12,54,128]{2,1,0:T(8,128)S(1)} collective-permute-done((f32[12,54,128]{2,1,0:T(8,128)S(1)}, f32[12,54,128]{2,1,0:T(8,128)S(1)}, u32[]{:S(2)}, u32[]{:S(2)}) %collective-permute-start.6) | collective-permute-done | bytes 331808 | tf_op jit(solution)/shard_map/ppermute | solution.py:386
  49.9 7.9 %shard_map.21 = f32[72,24,128]{2,1,0:T(8,128)S(1)} custom-call(f32[72,24,128]{2,1,0:T(8,128)S(1)} %get-tuple-element.8.u_ref.refs_0_, f32[72,24,128]{2,1,0:T(8,128)S(1)} %collective-permute-done.4.b_ref.refs_1_, f32[12,54,128]{2,1,0:T(8,128)S(1)} %collective-permute-done.5.refs_2_, f32[12,54,128]{2,1,0:T(8,128)S(1)} %collective-permute-done.6.refs_3_, ...), custom_call_target="tpu_custom_call" | custom-call | tf_op jit(solution)/shard_map/pallas_call | solution.py:363
  57.8 0.9 %reshape.7 = f32[1,1,72,2304]{3,2,1,0:T(8,128)} reshape(f32[72,18,128]{2,1,0:T(8,128)S(1)} %bitcast.3) | data formatting | bytes 1327104 | tf_op jit(solution)/shard_map/reshape | solution.py:415
  (3 shorter events, 0.1 us)
Async XLA Ops:
  1.3 6.2 %collective-permute-start = (f32[72,24,128]{2,1,0:T(8,128)S(1)}, f32[72,24,128]{2,1,0:T(8,128)S(1)}, u32[]{:S(2)}, u32[]{:S(2)}) collective-permute-start(f32[72,24,128]{2,1,0:T(8,128)S(1)} %pad.4.u_ref.refs_0_), channel_id=1, source_target_pairs={{0,1},{1,0},{2,3},{3,2},{4,5},{5,4},{6,7},{7,6},{8,9},{9,8},{10,11... | collective-permute-start | bytes 2654216 | tf_op jit(solution)/shard_map/ppermute | solution.py:378
  1.8 13.6 %collective-permute-start.1 = (f32[12,54,128]{2,1,0:T(8,128)S(1)}, f32[12,54,128]{2,1,0:T(8,128)S(1)}, u32[]{:S(2)}, u32[]{:S(2)}) collective-permute-start(f32[12,54,128]{2,1,0:T(8,128)S(1)} %shard_map.17), channel_id=1, source_target_pairs={{2,0},{4,2},{6,4},{8,6},{10,8},{12,10},{14,12},{0,14},{3,1},{5,3},... | collective-permute-start | bytes 995336 | tf_op jit(solution)/shard_map/ppermute | solution.py:379
  8.5 12.9 %collective-permute-start.2 = (f32[12,54,128]{2,1,0:T(8,128)S(1)}, f32[12,54,128]{2,1,0:T(8,128)S(1)}, u32[]{:S(2)}, u32[]{:S(2)}) collective-permute-start(f32[12,54,128]{2,1,0:T(8,128)S(1)} %shard_map.18), channel_id=1, source_target_pairs={{0,2},{2,4},{4,6},{6,8},{8,10},{10,12},{12,14},{14,0},{1,3},{3,5},... | collective-permute-start | bytes 995336 | tf_op jit(solution)/shard_map/ppermute | solution.py:386
  15.4 1.4 %collective-permute-start.3 = (f32[12,18,128]{2,1,0:T(8,128)S(1)}, f32[12,18,128]{2,1,0:T(8,128)S(1)}, u32[]{:S(2)}, u32[]{:S(2)}) collective-permute-start(f32[12,18,128]{2,1,0:T(8,128)S(1)} %slice.12), channel_id=1, source_target_pairs={{0,1},{1,0},{2,3},{3,2},{4,5},{5,4},{6,7},{7,6},{8,9},{9,8},{10,11... | collective-permute-start | bytes 331784 | tf_op jit(solution)/shard_map/ppermute | solution.py:387
  29.3 6.7 %collective-permute-start.4 = (f32[72,24,128]{2,1,0:T(8,128)S(1)}, f32[72,24,128]{2,1,0:T(8,128)S(1)}, u32[]{:S(2)}, u32[]{:S(2)}) collective-permute-start(f32[72,24,128]{2,1,0:T(8,128)S(1)} %get-tuple-element.8.u_ref.refs_0_), channel_id=1, source_target_pairs={{0,1},{1,0},{2,3},{3,2},{4,5},{5,4},{6,7},{7,6},{8,9},{9,8},{10,11... | collective-permute-start | bytes 2654216 | tf_op jit(solution)/shard_map/ppermute | solution.py:378
  29.4 14.5 %collective-permute-start.5 = (f32[12,54,128]{2,1,0:T(8,128)S(1)}, f32[12,54,128]{2,1,0:T(8,128)S(1)}, u32[]{:S(2)}, u32[]{:S(2)}) collective-permute-start(f32[12,54,128]{2,1,0:T(8,128)S(1)} %get-tuple-element.9), channel_id=1, source_target_pairs={{2,0},{4,2},{6,4},{8,6},{10,8},{12,10},{14,12},{0,14},{3,1},{5,3},... | collective-permute-start | bytes 995336 | tf_op jit(solution)/shard_map/ppermute | solution.py:379
  37.1 12.9 %collective-permute-start.6 = (f32[12,54,128]{2,1,0:T(8,128)S(1)}, f32[12,54,128]{2,1,0:T(8,128)S(1)}, u32[]{:S(2)}, u32[]{:S(2)}) collective-permute-start(f32[12,54,128]{2,1,0:T(8,128)S(1)} %shard_map.20), channel_id=1, source_target_pairs={{0,2},{2,4},{4,6},{6,8},{8,10},{10,12},{12,14},{14,0},{1,3},{3,5},... | collective-permute-start | bytes 995336 | tf_op jit(solution)/shard_map/ppermute | solution.py:386
  43.9 1.4 %collective-permute-start.7 = (f32[12,18,128]{2,1,0:T(8,128)S(1)}, f32[12,18,128]{2,1,0:T(8,128)S(1)}, u32[]{:S(2)}, u32[]{:S(2)}) collective-permute-start(f32[12,18,128]{2,1,0:T(8,128)S(1)} %slice.13), channel_id=1, source_target_pairs={{0,1},{1,0},{2,3},{3,2},{4,5},{5,4},{6,7},{7,6},{8,9},{9,8},{10,11... | collective-permute-start | bytes 331784 | tf_op jit(solution)/shard_map/ppermute | solution.py:387

commit v2 on v1

v2 whole, which is shorter than its diff:
```python
import jax
import jax.numpy as jnp
from jax import lax
from jax.experimental import pallas as pl
from jax.experimental.pallas import tpu as pltpu
from jax.sharding import PartitionSpec as P

X = 48
ROWS = 18
LANES = 128
PAD = 24
BASE = 8
HALO = 32
flow_step = 0.05


def dot3(lefts, rights, conj_left, conj_right, want=(True, True)):
    real = imag = None
    for (ar, ai), (br, bi) in zip(lefts, rights):
        if want[0]:
            first = ar * br
            second = ai * bi
            term = first + second if conj_left != conj_right else first - second
            real = term if real is None else real + term
        if want[1]:
            first = ar * bi
            second = ai * br
            if conj_left and conj_right:
                term = -(first + second)
            elif conj_left:
                term = first - second
            elif conj_right:
                term = second - first
            else:
                term = first + second
            imag = term if imag is None else imag + term
    return real, imag


def product(a, b, adj_a=False, adj_b=False, rows=3):
    out = []
    for i in range(rows):
        left = [a[k][i] if adj_a else a[i][k] for k in range(3)]
        out.append(
            [
                dot3(left, [b[j][k] if adj_b else b[k][j] for k in range(3)], adj_a, adj_b)
                for j in range(3)
            ]
        )
    return out


def antiherm_product(a, b, adj_b=False):
    def entry(i, j, want=(True, True)):
        return dot3(
            [a[i][k] for k in range(3)],
            [b[j][k] if adj_b else b[k][j] for k in range(3)],
            False,
            adj_b,
            want,
        )

    out = []
    for i in range(3):
        value = entry(i, i, (False, True))[1]
        out.append(value + value)
    for i, j in ((0, 1), (0, 2), (1, 2)):
        up = entry(i, j)
        low = entry(j, i)
        out.append(up[0] - low[0])
        out.append(up[1] + low[1])
    return out


def third_row(rows):
    a, b = rows
    out = []
    for j in range(3):
        k, m = (j + 1) % 3, (j + 2) % 3
        (pr, pi), (qr, qi) = a[k], b[m]
        (sr, si), (tr, ti) = a[m], b[k]
        out.append(
            ((pr * qr - pi * qi) - (sr * tr - si * ti), (sr * ti + si * tr) - (pr * qi + pi * qr))
        )
    return out


def expmap(q):
    d = q[:3]
    h = [(q[4], -q[3]), (q[6], -q[5]), (q[8], -q[7])]
    n = [r * r + i * i for r, i in h]
    s = [
        d[0] * d[0] + n[0] + n[1],
        d[1] * d[1] + n[0] + n[2],
        d[2] * d[2] + n[1] + n[2],
    ]
    (ar, ai), (br, bi), (cr, ci) = h
    e01 = d[0] + d[1]
    e02 = d[0] + d[2]
    e12 = d[1] + d[2]
    w_r = ar * cr - ai * ci
    w_i = ar * ci + ai * cr
    so = [
        (e01 * ar + (br * cr + bi * ci), e01 * ai + (bi * cr - br * ci)),
        (e02 * br + w_r, e02 * bi + w_i),
        (e12 * cr + (ar * br + ai * bi), e12 * ci + (ar * bi - ai * br)),
    ]
    p = 0.5 * (s[0] + s[1] + s[2])
    det = (
        d[0] * d[1] * d[2]
        + 2.0 * (w_r * br + w_i * bi)
        - d[0] * n[2]
        - d[1] * n[1]
        - d[2] * n[0]
    )
    dd = det * det
    pp = p * p
    top = dd + pp * p
    f0r = 1.0 - dd * (1.0 / 720.0 - p * (2.0 / 40320.0))
    f1r = det * (1.0 / 24.0 - p * (2.0 / 720.0) + pp * (3.0 / 40320.0))
    f2r = -0.5 + p * (1.0 / 24.0) - pp * (1.0 / 720.0) + top * (1.0 / 40320.0)
    f0i = det * (-1.0 / 6.0 + p * (1.0 / 120.0) - pp * (1.0 / 5040.0))
    f1i = 1.0 - p * (1.0 / 6.0) + pp * (1.0 / 120.0) - top * (1.0 / 5040.0)
    f2i = det * (1.0 / 120.0 - p * (2.0 / 5040.0))
    out = [[None] * 3 for _ in range(3)]
    for i in range(3):
        out[i][i] = (f0r + f1r * d[i] + f2r * s[i], f0i + f1i * d[i] + f2i * s[i])
    for (i, j), (hr, hi), (sr, si) in zip(((0, 1), (0, 2), (1, 2)), h, so):
        rr = f1r * hr + f2r * sr
        ii = f1i * hi + f2i * si
        ri = f1r * hi + f2r * si
        ir = f1i * hr + f2i * sr
        out[i][j] = (rr - ii, ri + ir)
        out[j][i] = (rr + ii, ir - ri)
    return out


def load(ref, mat, rows, count=3):
    return [
        [
            (ref[mat * 18 + (i * 3 + j) * 2, rows, :], ref[mat * 18 + (i * 3 + j) * 2 + 1, rows, :])
            for j in range(3)
        ]
        for i in range(count)
    ]


def store(ref, base, rows, matrix):
    for i, row in enumerate(matrix):
        for j, (re, im) in enumerate(row):
            ref[base + (i * 3 + j) * 2, rows, :] = re
            ref[base + (i * 3 + j) * 2 + 1, rows, :] = im


def wrap_rows(ref, mat, count):
    span = slice(mat * 18, (mat + count) * 18)
    ref[span, BASE - 1 : BASE, :] = ref[span, BASE + ROWS - 1 : BASE + ROWS, :]
    ref[span, BASE + ROWS : BASE + ROWS + 1, :] = ref[span, BASE : BASE + 1, :]


def shift_value(here, after, before, step, lane, column):
    if step == "+y":
        return pltpu.roll(jnp.where(lane >= X, here, after), LANES - X, 1)
    if step == "-y":
        return pltpu.roll(jnp.where(lane < LANES - X, here, before), X, 1)
    if step == "+x":
        near = pltpu.roll(jnp.where(lane >= 1, here, after), LANES - 1, 1)
        far = pltpu.roll(jnp.where(lane < LANES - X + 1, here, before), X - 1, 1)
        return jnp.where(column == X - 1, far, near)
    near = pltpu.roll(jnp.where(lane < LANES - 1, here, before), 1, 1)
    far = pltpu.roll(jnp.where(lane >= X - 1, here, after), LANES - X + 1, 1)
    return jnp.where(column == 0, far, near)


def shift_matrices(source, source_mat, target, target_mat, count, step):
    lane = lax.broadcasted_iota(jnp.int32, (ROWS, LANES), 1)
    row = lax.broadcasted_iota(jnp.int32, (ROWS, LANES), 0)
    column = lax.rem(row * LANES + lane, X)

    def body(group, carry):
        for inner in range(6):
            index = group * 6 + inner
            here = source[source_mat * 18 + index, BASE : BASE + ROWS, :]
            after = source[source_mat * 18 + index, BASE + 1 : BASE + ROWS + 1, :]
            before = source[source_mat * 18 + index, BASE - 1 : BASE + ROWS - 1, :]
            target[target_mat * 18 + index, 0:ROWS, :] = shift_value(
                here, after, before, step, lane, column
            )
        return carry

    lax.fori_loop(0, count * 3, body, 0)


KEPT = (0, 1, 3, 4, 5, 6, 7, 8)


def load_nine(ref, base, rows):
    kept = [ref[base + k, rows, :] for k in range(8)]
    return kept[:2] + [-(kept[0] + kept[1])] + kept[2:]


def traceless(loop):
    mean = (loop[0] + loop[1] + loop[2]) * (1.0 / 3.0)
    return [loop[k] - mean if k < 3 else loop[k] for k in range(9)]


def add_matrices(first, other):
    return [
        [(a[0] + b[0], a[1] + b[1]) for a, b in zip(ra, rb)] for ra, rb in zip(first, other)
    ]


def chunks(body):
    def step(chunk, carry):
        rows = pl.ds(pl.multiple_of(chunk * 8, 8), 8)
        inner = pl.ds(pl.multiple_of(chunk * 8 + BASE, 8), 8)
        body(rows, inner)
        return carry

    lax.fori_loop(0, 3, step, 0)


def pack_rows(target, slot, source, entries):
    for position, entry in enumerate(entries):
        target[slot, position * ROWS : (position + 1) * ROWS, :] = source[entry, 0:ROWS, :]


def unpack_rows(source, slot, target, base, count):
    for e in range(count):
        target[base + e, 0:ROWS, :] = source[slot, e * ROWS : (e + 1) * ROWS, :]


def section_kernel(second, *refs):
    if second:
        u_ref, d_ref, halo_in, out_ref = refs[:4]
        refs = refs[4:]
    else:
        u_ref, out_ref, drift_ref, halo_out = refs[:4]
        refs = refs[4:]
    (field, sib, zfield, fx, fy, halo, corner, carried, low, lowm, staple, force,
     face_send, face_recv, loop_send, loop_recv, loops, arrived, send_sem, recv_sem) = refs
    if not second:
        halo = halo_out
    count = lax.axis_size("ta")
    time = lax.axis_index("ta")
    after = {"ta": lax.rem(time + 1, count)}
    before = {"ta": lax.rem(time + count - 1, count)}
    partner = {"gz": 1 - lax.axis_index("gz")}

    barrier = pltpu.get_barrier_semaphore()
    for device in (after, before, partner):
        pl.semaphore_signal(barrier, inc=1, device_id=device, device_id_type=pl.DeviceIdType.MESH)

    def remote(source, target, index, device):
        return pltpu.make_async_remote_copy(
            src_ref=source,
            dst_ref=target,
            send_sem=send_sem.at[index],
            recv_sem=recv_sem.at[index],
            device_id=device,
            device_id_type=pl.DeviceIdType.MESH,
        )

    for d in range(3):
        if second:
            pack_rows(face_send, d, d_ref, [(d + 1) * 9 + k for k in KEPT])
        else:
            pack_rows(face_send, d, u_ref, range((d + 1) * 18, (d + 1) * 18 + 12))
    pl.semaphore_wait(barrier, 3)
    faces = [remote(face_send.at[d], face_recv.at[d], 1 + d, before) for d in range(3)]
    whole = remote(u_ref, sib, 0, partner)
    whole.start()
    for copy in faces:
        copy.start()

    field[:, BASE : BASE + ROWS, :] = u_ref[:, 0:ROWS, :]
    wrap_rows(field, 0, 4)
    shift_matrices(field, 0, fx, 0, 3, "+x")
    shift_matrices(field, 0, fy, 0, 2, "+y")
    shift_matrices(field, 3, fy, 2, 1, "+y")

    whole.wait_recv()
    zfield[:, BASE : BASE + ROWS, :] = sib[18:36, 0:ROWS, :]
    wrap_rows(zfield, 0, 1)
    shift_matrices(zfield, 0, fx, 3, 1, "+x")
    shift_matrices(zfield, 0, fy, 3, 1, "+y")

    def transport(rows, inner):
        time_link = load(u_ref, 0, rows)
        for d in range(3):
            ahead = load((sib, fy, fx)[d], 0, rows)
            right = product(load(u_ref, d + 1, rows), ahead)
            store(carried, d * 18, rows, product(time_link, right, adj_a=True))

    chunks(transport)

    def link(mu, nu, rows):
        if nu == 0:
            return load(halo, mu - 1, rows)
        if nu == 1:
            return load(sib, mu, rows)
        if nu == 2:
            return load(fy, {0: 0, 1: 1, 3: 2}[mu], rows)
        return load(fx, mu, rows)

    def plane(mu, nu, totals, rows, inner):
        first = load(u_ref, mu, rows)
        other = load(u_ref, nu, rows)
        near = product(first, link(nu, mu, rows))
        far = product(other, link(mu, nu, rows))
        loop = antiherm_product(near, far, adj_b=True)
        for which, sign in ((mu, 1), (nu, -1)):
            old = totals[which]
            if old is None:
                totals[which] = loop if sign == 1 else [-b for b in loop]
            elif sign == 1:
                totals[which] = [a + b for a, b in zip(old, loop)]
            else:
                totals[which] = [a - b for a, b in zip(old, loop)]
        if nu == 2:
            store(low, (3 + mu) * 18, inner, product(near, other, adj_a=True))
        if nu == 3:
            store(low, mu * 18, inner, product(near, other, adj_a=True))
        if (mu, nu) == (2, 3):
            store(low, 5 * 18, inner, product(far, first, adj_a=True))

    def space_planes(rows, inner):
        totals = [None] * 4
        for mu, nu in ((1, 2), (1, 3), (2, 3)):
            plane(mu, nu, totals, rows, inner)
        for mu in range(1, 4):
            for k in range(9):
                force[mu * 9 + k, rows, :] = totals[mu][k]
        for mu in (2, 3):
            right = product(load(sib, mu, rows), load(sib, 1, rows), adj_a=True)
            ahead = load((fy, fx)[mu - 2], 3, rows)
            store(staple, mu * 18, rows, product(ahead, right, adj_a=True))
        store(staple, 0, rows, product(load(sib, 0, rows), load(sib, 1, rows), adj_a=True))

    chunks(space_planes)
    wrap_rows(low, 1, 2)
    wrap_rows(low, 4, 2)
    shift_matrices(low, 1, lowm, 1, 2, "-x")
    shift_matrices(low, 4, lowm, 4, 2, "-y")

    sends = []
    edge = remote(halo.at[pl.ds(0, 18)], corner, 7, partner)
    for d in range(3):
        faces[d].wait_recv()
        if second:
            unpack_rows(face_recv, d, arrived, d * 8, 8)
        else:
            unpack_rows(face_recv, d, halo, d * 18, 12)

        def rebuild(rows, inner):
            if second:
                drift = load_nine(arrived, d * 8, rows)
                moved = product(expmap([0.25 * v for v in drift]), load(halo_in, d, rows))
                store(halo, d * 18, rows, moved)
            else:
                moved = load(halo, d, rows, 2)
                moved.append(third_row(moved))
                store(halo, d * 18 + 12, rows, moved[2:])
            loop = traceless(antiherm_product(moved, load(carried, d, rows), adj_b=True))
            for position, k in enumerate(KEPT):
                loops[d * 8 + position, rows, :] = loop[k]

        chunks(rebuild)
        pack_rows(loop_send, d, loops, range(d * 8, d * 8 + 8))
        sends.append(remote(loop_send.at[d], loop_recv.at[d], 4 + d, after))
        sends[d].start()
        if d == 0:
            edge.start()

    def time_planes(rows, inner):
        totals = [None] + [[force[mu * 9 + k, rows, :] for k in range(9)] for mu in range(1, 4)]
        for nu in range(1, 4):
            plane(0, nu, totals, rows, inner)
        for mu in range(4):
            for k in range(9):
                force[mu * 9 + k, rows, :] = totals[mu][k]

    chunks(time_planes)
    wrap_rows(low, 0, 1)
    wrap_rows(low, 3, 1)
    shift_matrices(low, 0, lowm, 0, 1, "-x")
    shift_matrices(low, 3, lowm, 3, 1, "-y")
    edge.wait_recv()

    def lower_loops(rows, inner):
        for mu in range(4):
            parts = []
            if mu == 0:
                parts.append(product(load(corner, 0, rows), load(staple, 0, rows), adj_a=True))
            elif mu != 1:
                parts.append(load(staple, mu, rows))
            if mu != 3:
                parts.append(load(lowm, mu, rows))
            if mu != 2:
                parts.append(load(lowm, {0: 3, 1: 4, 3: 5}[mu], rows))
            total = parts[0]
            for part in parts[1:]:
                total = add_matrices(total, part)
            loop = antiherm_product(load(u_ref, mu, rows), total)
            for k in range(9):
                force[mu * 9 + k, rows, :] += loop[k]

    chunks(lower_loops)

    def finish_link(mu, rows):
        loop = [force[mu * 9 + k, rows, :] for k in range(9)]
        if mu != 0:
            extra = load_nine(arrived, (mu - 1) * 8, rows)
            loop = [a + b for a, b in zip(loop, extra)]
        loop = traceless(loop)
        if second:
            generator = [
                loop[k] * (-0.5 * flow_step * 8.0 / 9.0)
                - (17.0 / 36.0) * d_ref[mu * 9 + k, rows, :]
                for k in range(9)
            ]
        else:
            drift = [value * (-0.5 * flow_step) for value in loop]
            for k in range(9):
                drift_ref[mu * 9 + k, rows, :] = drift[k]
            generator = [0.25 * value for value in drift]
        store(out_ref, mu * 18, rows, product(expmap(generator), load(u_ref, mu, rows)))

    chunks(lambda rows, inner: finish_link(0, rows))
    for d in range(3):
        sends[d].wait_recv()
        unpack_rows(loop_recv, d, arrived, d * 8, 8)
        chunks(lambda rows, inner: finish_link(d + 1, rows))
    for copy in [whole, edge] + faces + sends:
        copy.wait_send()


VM = pl.BlockSpec(memory_space=pltpu.VMEM)


def f32(*shape):
    return jax.ShapeDtypeStruct(shape, jnp.float32)


def section(inputs, outs, second):
    face = (8 if second else 12) * ROWS
    shapes = [
        (72, HALO, LANES),
        (72, PAD, LANES),
        (18, HALO, LANES),
        (72, PAD, LANES),
        (72, PAD, LANES),
        (54 if second else 1, PAD, LANES),
        (18, PAD, LANES),
        (54, PAD, LANES),
        (108, HALO, LANES),
        (108, PAD, LANES),
        (72, PAD, LANES),
        (36, PAD, LANES),
        (3, face, LANES),
        (3, face, LANES),
        (3, 8 * ROWS, LANES),
        (3, 8 * ROWS, LANES),
        (24, PAD, LANES),
        (24, PAD, LANES),
    ]

    def kernel(*refs):
        section_kernel(second, *refs)

    return pl.pallas_call(
        kernel,
        out_shape=outs,
        in_specs=[VM] * len(inputs),
        out_specs=jax.tree.map(lambda _: VM, outs),
        scratch_shapes=[pltpu.VMEM(shape, jnp.float32) for shape in shapes]
        + [pltpu.SemaphoreType.DMA((8,)), pltpu.SemaphoreType.DMA((8,))],
        compiler_params=pltpu.CompilerParams(
            vmem_limit_bytes=40 * 2**20,
            collective_id=int(second),
            has_side_effects=True,
        ),
    )(*inputs)


def shards(links):
    full_shape = links.shape
    first = jnp.pad(links.reshape(72, ROWS, LANES), ((0, 0), (0, PAD - ROWS), (0, 0)))
    middle, drift, halo = section(
        [first], [f32(72, PAD, LANES), f32(36, PAD, LANES), f32(54, PAD, LANES)], False
    )
    result = section([middle, drift, halo], f32(72, PAD, LANES), True)
    return result[:, :ROWS].reshape(full_shape)


def solution(mesh):
    in_specs = (P(("cfg", "ta"), "gz", None, None),)
    out_specs = P(("cfg", "ta"), "gz", None, None)
    return jax.shard_map(shards, mesh=mesh, in_specs=in_specs, out_specs=out_specs, check_vma=False)
```

time: 59.7 us -> 40.7 us (0.68); the launches traced: 58.8 us -> 40.5 us
  waiting for transfers between devices: 25.5 us -> 0 us
  Pallas kernels: 17.9 us -> 38.3 us
  starting transfers between devices: 13.1 us -> 0 us
    ppermute x8 -> x0, waiting for transfers between devices: 25.5 us -> none  [the longest x2 13.7 us: section(): ahead = lax.ppermute(pack, 'ta', backward)]
    pallas_call x5 -> x2, Pallas kernels: 17.9 us -> 38.3 us  [section(): pl.pallas_call(kernel, out_shape=outs, in_specs=[VM] * len(inputs), out_s...]
    ppermute x8 -> x0, starting transfers between devices: 13.1 us -> none  [the longest x2 12.2 us: section(): ahead = lax.ppermute(pack, 'ta', backward)]
  transfers between devices with their start and end apart: 8 -> 0, of which waited for: 6 -> 0; matrix products, arithmetic and copies ran while one was open for 0% -> 0% of each run, Pallas kernels for 4% -> 0%
where the time goes in v2:
time: 40.7 us; the launch traced here: 40.5 us
  Pallas kernels  38.3 us (94%)
  local copies, waits for them, and re-layouts  2.19 us (5%)
    pallas_call x2, Pallas kernels, section(): pl.pallas_call(kernel, out_shape=outs, in_specs=[VM] * len(inputs), out_s...  38.3 us
    reshape x1, local copies, waits for them, and re-layouts, shards(): links.reshape(72, ROWS, LANES)  1.18 us
    reshape x1, local copies, waits for them, and re-layouts, shards(): return result[:, :ROWS].reshape(full_shape)  0.95 us

profile of v2, /device:TPU:0, one launch (start us, length us, event | category | flops | bytes accessed | tf_op | source)
XLA Modules:
  0.0 40.5 jit_solution(16809016703508653876)
XLA Ops:
  0.0 1.2 %reshape.6 = f32[72,18,128]{2,1,0:T(8,128)S(1)} reshape(f32[1,1,72,2304]{3,2,1,0:T(8,128)} %param.1) | data formatting | bytes 1327104 | tf_op jit(solution)/shard_map/reshape | solution.py:488
  1.2 0.1 pad.4.refs_0_
  1.3 21.2 %shard_map.17 = (f32[72,24,128]{2,1,0:T(8,128)S(1)}, f32[36,24,128]{2,1,0:T(8,128)S(1)}, f32[54,24,128]{2,1,0:T(8,128)S(1)}) custom-call(f32[72,24,128]{2,1,0:T(8,128)S(1)} %pad.4.refs_0_), custom_call_target="tpu_custom_call" | custom-call | tf_op jit(solution)/shard_map/pallas_call | solution.py:471
  22.5 17.1 %shard_map.18 = f32[72,24,128]{2,1,0:T(8,128)S(1)} custom-call(f32[72,24,128]{2,1,0:T(8,128)S(1)} %get-tuple-element.8.refs_0_, f32[36,24,128]{2,1,0:T(8,128)S(1)} %get-tuple-element.9.refs_1_, f32[54,24,128]{2,1,0:T(8,128)S(1)} %get-tuple-element.10.refs_2_), custom_call_target="tpu_custom_call" | custom-call | tf_op jit(solution)/shard_map/pallas_call | solution.py:471
  39.6 0.9 %reshape.7 = f32[1,1,72,2304]{3,2,1,0:T(8,128)} reshape(f32[72,18,128]{2,1,0:T(8,128)S(1)} %bitcast.3) | data formatting | bytes 1327104 | tf_op jit(solution)/shard_map/reshape | solution.py:493

commit v3 on v2

--- a/solution.py
+++ b/solution.py
@@ -230,17 +230,11 @@
         target[base + e, 0:ROWS, :] = source[slot, e * ROWS : (e + 1) * ROWS, :]
 
 
-def section_kernel(second, *refs):
-    if second:
-        u_ref, d_ref, halo_in, out_ref = refs[:4]
-        refs = refs[4:]
-    else:
-        u_ref, out_ref, drift_ref, halo_out = refs[:4]
-        refs = refs[4:]
-    (field, sib, zfield, fx, fy, halo, corner, carried, low, lowm, staple, force,
-     face_send, face_recv, loop_send, loop_recv, loops, arrived, send_sem, recv_sem) = refs
-    if not second:
-        halo = halo_out
+def flow_kernel(*refs):
+    links_ref, out_ref = refs[:2]
+    (middle, drift_ref, field, zfield, fx, fy, carried, low, lowm, staple, force, loops, arrived,
+     sib_a, sib_b, halo_a, halo_b, corner_a, corner_b, face_send_a, face_recv_a, face_send_b,
+     face_recv_b, loop_send_a, loop_recv_a, loop_send_b, loop_recv_b, send_sem, recv_sem) = refs[2:]
     count = lax.axis_size("ta")
     time = lax.axis_index("ta")
     after = {"ta": lax.rem(time + 1, count)}
@@ -261,17 +255,47 @@
             device_id_type=pl.DeviceIdType.MESH,
         )
 
+    def copies(section, u_ref, sib, halo, corner, face_send, face_recv, loop_send, loop_recv):
+        base = section * 11
+        whole = [
+            remote(u_ref.at[pl.ds(m * 18, 18)], sib.at[pl.ds(m * 18, 18)], base + m, partner)
+            for m in range(4)
+        ]
+        faces = [remote(face_send.at[d], face_recv.at[d], base + 4 + d, before) for d in range(3)]
+        sends = [remote(loop_send.at[d], loop_recv.at[d], base + 7 + d, after) for d in range(3)]
+        edge = remote(halo.at[pl.ds(0, 18)], corner, base + 10, partner)
+        return whole, faces, sends, edge
+
+    local = (field, zfield, fx, fy, carried, low, lowm, staple, force, loops, arrived, drift_ref)
+    set_a = (sib_a, halo_a, corner_a, face_send_a, face_recv_a, loop_send_a, loop_recv_a)
+    set_b = (sib_b, halo_b, corner_b, face_send_b, face_recv_b, loop_send_b, loop_recv_b)
+    first = copies(0, links_ref, *set_a)
+    second = copies(1, middle, *set_b)
+
     for d in range(3):
-        if second:
-            pack_rows(face_send, d, d_ref, [(d + 1) * 9 + k for k in KEPT])
-        else:
-            pack_rows(face_send, d, u_ref, range((d + 1) * 18, (d + 1) * 18 + 12))
+        pack_rows(face_send_a, d, links_ref, range((d + 1) * 18, (d + 1) * 18 + 12))
     pl.semaphore_wait(barrier, 3)
-    faces = [remote(face_send.at[d], face_recv.at[d], 1 + d, before) for d in range(3)]
-    whole = remote(u_ref, sib, 0, partner)
-    whole.start()
-    for copy in faces:
+    for copy in first[1] + first[0]:
         copy.start()
+
+    def announce(mu):
+        second[0][mu].start()
+        if mu:
+            pack_rows(face_send_b, mu - 1, drift_ref, [mu * 9 + k for k in KEPT])
+            second[1][mu - 1].start()
+
+    section(False, links_ref, middle, None, local, set_a, first, announce)
+    section(True, middle, out_ref, halo_a, local, set_b, second, lambda mu: None)
+    for whole, faces, sends, edge in (first, second):
+        for copy in whole + faces + sends + [edge]:
+            copy.wait_send()
+
+
+def section(second, u_ref, out_ref, halo_in, local, received, transfers, announce):
+    field, zfield, fx, fy, carried, low, lowm, staple, force, loops, arrived, drift_ref = local
+    sib, halo, corner, face_send, face_recv, loop_send, loop_recv = received
+    whole, faces, sends, edge = transfers
+    d_ref = drift_ref
 
     field[:, BASE : BASE + ROWS, :] = u_ref[:, 0:ROWS, :]
     wrap_rows(field, 0, 4)
@@ -279,7 +303,8 @@
     shift_matrices(field, 0, fy, 0, 2, "+y")
     shift_matrices(field, 3, fy, 2, 1, "+y")
 
-    whole.wait_recv()
+    for copy in whole[:2]:
+        copy.wait_recv()
     zfield[:, BASE : BASE + ROWS, :] = sib[18:36, 0:ROWS, :]
     wrap_rows(zfield, 0, 1)
     shift_matrices(zfield, 0, fx, 3, 1, "+x")
@@ -293,6 +318,8 @@
             store(carried, d * 18, rows, product(time_link, right, adj_a=True))
 
     chunks(transport)
+    for copy in whole[2:]:
+        copy.wait_recv()
 
     def link(mu, nu, rows):
         if nu == 0:
@@ -343,8 +370,6 @@
     shift_matrices(low, 1, lowm, 1, 2, "-x")
     shift_matrices(low, 4, lowm, 4, 2, "-y")
 
-    sends = []
-    edge = remote(halo.at[pl.ds(0, 18)], corner, 7, partner)
     for d in range(3):
         faces[d].wait_recv()
         if second:
@@ -367,7 +392,6 @@
 
         chunks(rebuild)
         pack_rows(loop_send, d, loops, range(d * 8, d * 8 + 8))
-        sends.append(remote(loop_send.at[d], loop_recv.at[d], 4 + d, after))
         sends[d].start()
         if d == 0:
             edge.start()
@@ -427,12 +451,12 @@
         store(out_ref, mu * 18, rows, product(expmap(generator), load(u_ref, mu, rows)))
 
     chunks(lambda rows, inner: finish_link(0, rows))
+    announce(0)
     for d in range(3):
         sends[d].wait_recv()
         unpack_rows(loop_recv, d, arrived, d * 8, 8)
         chunks(lambda rows, inner: finish_link(d + 1, rows))
-    for copy in [whole, edge] + faces + sends:
-        copy.wait_send()
+        announce(d + 1)
 
 
 VM = pl.BlockSpec(memory_space=pltpu.VMEM)
@@ -442,55 +466,55 @@
     return jax.ShapeDtypeStruct(shape, jnp.float32)
 
 
-def section(inputs, outs, second):
-    face = (8 if second else 12) * ROWS
+def flow(links):
+    face = (3, 12 * ROWS, LANES)
+    short = (3, 8 * ROWS, LANES)
     shapes = [
+        (72, PAD, LANES),
+        (36, PAD, LANES),
         (72, HALO, LANES),
-        (72, PAD, LANES),
         (18, HALO, LANES),
         (72, PAD, LANES),
         (72, PAD, LANES),
-        (54 if second else 1, PAD, LANES),
-        (18, PAD, LANES),
         (54, PAD, LANES),
         (108, HALO, LANES),
         (108, PAD, LANES),
         (72, PAD, LANES),
         (36, PAD, LANES),
-        (3, face, LANES),
-        (3, face, LANES),
-        (3, 8 * ROWS, LANES),
-        (3, 8 * ROWS, LANES),
         (24, PAD, LANES),
         (24, PAD, LANES),
+        (72, PAD, LANES),
+        (72, PAD, LANES),
+        (54, PAD, LANES),
+        (54, PAD, LANES),
+        (18, PAD, LANES),
+        (18, PAD, LANES),
+        face,
+        face,
+        short,
+        short,
+        short,
+        short,
+        short,
+        short,
     ]
-
-    def kernel(*refs):
-        section_kernel(second, *refs)
-
     return pl.pallas_call(
-        kernel,
-        out_shape=outs,
-        in_specs=[VM] * len(inputs),
-        out_specs=jax.tree.map(lambda _: VM, outs),
+        flow_kernel,
+        out_shape=f32(72, PAD, LANES),
+        in_specs=[VM],
+        out_specs=VM,
         scratch_shapes=[pltpu.VMEM(shape, jnp.float32) for shape in shapes]
-        + [pltpu.SemaphoreType.DMA((8,)), pltpu.SemaphoreType.DMA((8,))],
+        + [pltpu.SemaphoreType.DMA((22,)), pltpu.SemaphoreType.DMA((22,))],
         compiler_params=pltpu.CompilerParams(
-            vmem_limit_bytes=40 * 2**20,
-            collective_id=int(second),
-            has_side_effects=True,
+            vmem_limit_bytes=40 * 2**20, collective_id=0, has_side_effects=True
         ),
-    )(*inputs)
+    )(links)
 
 
 def shards(links):
     full_shape = links.shape
     first = jnp.pad(links.reshape(72, ROWS, LANES), ((0, 0), (0, PAD - ROWS), (0, 0)))
-    middle, drift, halo = section(
-        [first], [f32(72, PAD, LANES), f32(36, PAD, LANES), f32(54, PAD, LANES)], False
-    )
-    result = section([middle, drift, halo], f32(72, PAD, LANES), True)
-    return result[:, :ROWS].reshape(full_shape)
+    return flow(first)[:, :ROWS].reshape(full_shape)
 
 
 def solution(mesh):

time: 40.7 us -> 39.3 us (0.966)
  Pallas kernels: 38.3 us -> 36.9 us
    pallas_call x2 -> x1, Pallas kernels: 38.3 us -> 36.9 us  [flow(): pl.pallas_call(flow_kernel, out_shape=f32(72, PAD, LANES), in_specs=[VM],...]
where the time goes in v3:
time: 39.3 us; the launch traced here: 39.2 us
  Pallas kernels  36.9 us (94%)
  local copies, waits for them, and re-layouts  2.19 us (6%)
    pallas_call x1, Pallas kernels, flow(): pl.pallas_call(flow_kernel, out_shape=f32(72, PAD, LANES), in_specs=[VM],...  36.9 us
    reshape x1, local copies, waits for them, and re-layouts, shards(): links.reshape(72, ROWS, LANES)  1.18 us
    reshape x1, local copies, waits for them, and re-layouts, shards(): return flow(first)[:, :ROWS].reshape(full_shape)  0.95 us

profile of v3, /device:TPU:0, one launch (start us, length us, event | category | flops | bytes accessed | tf_op | source)
XLA Modules:
  0.0 39.2 jit_solution(3291641537766155091)
XLA Ops:
  0.0 1.2 %reshape.6 = f32[72,18,128]{2,1,0:T(8,128)S(1)} reshape(f32[1,1,72,2304]{3,2,1,0:T(8,128)} %param.1) | data formatting | bytes 1327104 | tf_op jit(solution)/shard_map/reshape | solution.py:516
  1.2 0.1 pad.4.refs_0_
  1.3 36.9 %shard_map.17 = f32[72,24,128]{2,1,0:T(8,128)S(1)} custom-call(f32[72,24,128]{2,1,0:T(8,128)S(1)} %pad.4.refs_0_), custom_call_target="tpu_custom_call" | custom-call | tf_op jit(solution)/shard_map/pallas_call | solution.py:501
  38.2 0.9 %reshape.7 = f32[1,1,72,2304]{3,2,1,0:T(8,128)} reshape(f32[72,18,128]{2,1,0:T(8,128)S(1)} %bitcast.3) | data formatting | bytes 1327104 | tf_op jit(solution)/shard_map/reshape | solution.py:517

commit v4 on v3

--- a/solution.py
+++ b/solution.py
@@ -234,7 +234,7 @@
     links_ref, out_ref = refs[:2]
     (middle, drift_ref, field, zfield, fx, fy, carried, low, lowm, staple, force, loops, arrived,
      sib_a, sib_b, halo_a, halo_b, corner_a, corner_b, face_send_a, face_recv_a, face_send_b,
-     face_recv_b, loop_send_a, loop_recv_a, loop_send_b, loop_recv_b, send_sem, recv_sem) = refs[2:]
+     face_recv_b, loop_send_a, loop_recv_a, loop_send_b, loop_recv_b, carry_send, carry_recv, send_sem, recv_sem) = refs[2:]
     count = lax.axis_size("ta")
     time = lax.axis_index("ta")
     after = {"ta": lax.rem(time + 1, count)}
@@ -271,6 +271,7 @@
     set_b = (sib_b, halo_b, corner_b, face_send_b, face_recv_b, loop_send_b, loop_recv_b)
     first = copies(0, links_ref, *set_a)
     second = copies(1, middle, *set_b)
+    first[2][2] = remote(carry_send, carry_recv, 9, after)
 
     for d in range(3):
         pack_rows(face_send_a, d, links_ref, range((d + 1) * 18, (d + 1) * 18 + 12))
@@ -284,14 +285,15 @@
             pack_rows(face_send_b, mu - 1, drift_ref, [mu * 9 + k for k in KEPT])
             second[1][mu - 1].start()
 
-    section(False, links_ref, middle, None, local, set_a, first, announce)
-    section(True, middle, out_ref, halo_a, local, set_b, second, lambda mu: None)
+    carry = (carry_send, carry_recv)
+    section(False, links_ref, middle, None, local, set_a, first, announce, carry)
+    section(True, middle, out_ref, halo_a, local, set_b, second, lambda mu: None, carry)
     for whole, faces, sends, edge in (first, second):
         for copy in whole + faces + sends + [edge]:
             copy.wait_send()
 
 
-def section(second, u_ref, out_ref, halo_in, local, received, transfers, announce):
+def section(second, u_ref, out_ref, halo_in, local, received, transfers, announce, carry):
     field, zfield, fx, fy, carried, low, lowm, staple, force, loops, arrived, drift_ref = local
     sib, halo, corner, face_send, face_recv, loop_send, loop_recv = received
     whole, faces, sends, edge = transfers
@@ -318,6 +320,9 @@
             store(carried, d * 18, rows, product(time_link, right, adj_a=True))
 
     chunks(transport)
+    if not second:
+        pack_rows(carry[0], 0, carried, range(36, 48))
+        sends[2].start()
     for copy in whole[2:]:
         copy.wait_recv()
 
@@ -386,13 +391,16 @@
                 moved = load(halo, d, rows, 2)
                 moved.append(third_row(moved))
                 store(halo, d * 18 + 12, rows, moved[2:])
+            if d == 2 and not second:
+                return
             loop = traceless(antiherm_product(moved, load(carried, d, rows), adj_b=True))
             for position, k in enumerate(KEPT):
                 loops[d * 8 + position, rows, :] = loop[k]
 
         chunks(rebuild)
-        pack_rows(loop_send, d, loops, range(d * 8, d * 8 + 8))
-        sends[d].start()
+        if second or d < 2:
+            pack_rows(loop_send, d, loops, range(d * 8, d * 8 + 8))
+            sends[d].start()
         if d == 0:
             edge.start()
 
@@ -433,7 +441,12 @@
 
     def finish_link(mu, rows):
         loop = [force[mu * 9 + k, rows, :] for k in range(9)]
-        if mu != 0:
+        if mu == 3 and not second:
+            moved = load(carried, 2, rows, 2)
+            moved.append(third_row(moved))
+            extra = antiherm_product(load(u_ref, 3, rows), moved, adj_b=True)
+            loop = [a + b for a, b in zip(loop, extra)]
+        elif mu != 0:
             extra = load_nine(arrived, (mu - 1) * 8, rows)
             loop = [a + b for a, b in zip(loop, extra)]
         loop = traceless(loop)
@@ -454,7 +467,10 @@
     announce(0)
     for d in range(3):
         sends[d].wait_recv()
-        unpack_rows(loop_recv, d, arrived, d * 8, 8)
+        if second or d < 2:
+            unpack_rows(loop_recv, d, arrived, d * 8, 8)
+        else:
+            unpack_rows(carry[1], 0, carried, 36, 12)
         chunks(lambda rows, inner: finish_link(d + 1, rows))
         announce(d + 1)
 
@@ -497,6 +513,8 @@
         short,
         short,
         short,
+        (1, 12 * ROWS, LANES),
+        (1, 12 * ROWS, LANES),
     ]
     return pl.pallas_call(
         flow_kernel,

time: 39.3 us -> 43.5 us (1.11)
  Pallas kernels: 36.9 us -> 41.1 us
    pallas_call x1, Pallas kernels: 36.9 us -> 41.1 us  [flow(): pl.pallas_call(flow_kernel, out_shape=f32(72, PAD, LANES), in_specs=[VM],...]
where the time goes in v4:
time: 43.5 us; the launch traced here: 43.3 us
  Pallas kernels  41.1 us (94%)
  local copies, waits for them, and re-layouts  2.19 us (5%)
    pallas_call x1, Pallas kernels, flow(): pl.pallas_call(flow_kernel, out_shape=f32(72, PAD, LANES), in_specs=[VM],...  41.1 us
    reshape x1, local copies, waits for them, and re-layouts, shards(): links.reshape(72, ROWS, LANES)  1.18 us
    reshape x1, local copies, waits for them, and re-layouts, shards(): return flow(first)[:, :ROWS].reshape(full_shape)  0.95 us

profile of v4, /device:TPU:0, one launch (start us, length us, event | category | flops | bytes accessed | tf_op | source)
XLA Modules:
  0.0 43.3 jit_solution(13352527041356299709)
XLA Ops:
  0.0 1.2 %reshape.6 = f32[72,18,128]{2,1,0:T(8,128)S(1)} reshape(f32[1,1,72,2304]{3,2,1,0:T(8,128)} %param.1) | data formatting | bytes 1327104 | tf_op jit(solution)/shard_map/reshape | solution.py:534
  1.2 0.1 pad.4.refs_0_
  1.3 41.1 %shard_map.17 = f32[72,24,128]{2,1,0:T(8,128)S(1)} custom-call(f32[72,24,128]{2,1,0:T(8,128)S(1)} %pad.4.refs_0_), custom_call_target="tpu_custom_call" | custom-call | tf_op jit(solution)/shard_map/pallas_call | solution.py:519
  42.4 0.9 %reshape.7 = f32[1,1,72,2304]{3,2,1,0:T(8,128)} reshape(f32[72,18,128]{2,1,0:T(8,128)S(1)} %bitcast.3) | data formatting | bytes 1327104 | tf_op jit(solution)/shard_map/reshape | solution.py:535
